TPU v7x, 256 devices: a whole 4x4x8 slice. The times are simulated.
256 devices in a mesh: seq: 32 (over x, z), head: 8 (over y, core).
Axes of the slice: x: 4, y: 4, z: 8, core: 2. Of those that a mesh axis runs over, the one named last changes fastest.
Arguments:
- inputs: bfloat16 [16384, 2048], P('seq'), may hold values from -11 to 11
- out_grad: bfloat16 [16384, 2048], P('seq'), may hold values from -6 to 6
- w_query: bfloat16 [2048, 1024], P(None, 'head'), may hold values from -1 to 1
- w_key: bfloat16 [2048, 512], P(None, 'head'), may hold values from -1 to 1
- w_value: bfloat16 [2048, 512], P(None, 'head'), may hold values from -0.125 to 0.125
- w_output: bfloat16 [1024, 2048], P('head'), may hold values from -0.1875 to 0.1875
Outputs:
- grad_inputs: bfloat16 [16384, 2048], P('seq', 'head')
- grad_query: float32 [2048, 1024], P('seq', 'head')
- grad_key: float32 [2048, 512], P('seq', 'head')
- grad_value: float32 [2048, 512], P('seq', 'head')
- grad_output: float32 [1024, 2048], P('head', 'seq')
All inputs are finite; a program needn't handle non-finite values.
Results may differ from a plain program's by a relative error of at most 0.04.
Values may be sent and summed in bfloat16 or wider, within the bound.
A program may use at most 64 MiB of HBM per device.

v0:
```python
import jax
import jax.numpy as jnp
from jax import lax
from jax.sharding import PartitionSpec as P

HQ = 16
HK = 8
HD = 64


ROPE_BASE = 500000.0
NEG_FILL = -1e30


def rotary(positions):
    half_dim = HD // 2
    frequency = ROPE_BASE ** (-(jnp.arange(half_dim, dtype=jnp.float32) * 2.0 / HD))
    angles = positions[:, None] * frequency[None, :]
    return (jnp.cos(angles), jnp.sin(angles))


def rotate(vectors, cos_table, sin_table):
    half_dim = vectors.shape[-1] // 2
    front_half, back_half = (vectors[..., :half_dim], vectors[..., half_dim:])
    return jnp.concatenate(
        [
            front_half * cos_table - back_half * sin_table,
            back_half * cos_table + front_half * sin_table,
        ],
        -1,
    )


def unrotate(vectors, cos_table, sin_table):
    half_dim = vectors.shape[-1] // 2
    front_half, back_half = (vectors[..., :half_dim], vectors[..., half_dim:])
    return jnp.concatenate(
        [
            front_half * cos_table + back_half * sin_table,
            back_half * cos_table - front_half * sin_table,
        ],
        -1,
    )


def attend(query_rows, dout_rows, first_row, kv_all, accumulator):
    row_count, kv_local, group_size, head_size = query_rows.shape
    scale_factor = head_size ** (-0.5)
    block_size = min(512, kv_all.shape[0])
    block_count = (first_row + row_count + block_size - 1) // block_size
    query_pos = first_row + jnp.arange(row_count, dtype=jnp.int32)

    def block_scores(block_id):
        kv_block = lax.dynamic_slice_in_dim(kv_all, block_id * block_size, block_size, 0)
        key_block = kv_block[..., :head_size]
        value_block = kv_block[..., head_size:]
        key_pos = block_id * block_size + jnp.arange(block_size, dtype=jnp.int32)
        raw_scores = (
            jnp.einsum("rkgd,ckd->kgrc", query_rows, key_block, preferred_element_type=jnp.float32)
            * scale_factor
        )
        visible = query_pos[:, None] >= key_pos[None, :]
        return (jnp.where(visible, raw_scores, NEG_FILL), key_block, value_block)

    def stat_step(block_id, carry):
        running_max, running_sum = carry
        scores, _, _ = block_scores(block_id)
        new_max = jnp.maximum(running_max, jnp.max(scores, axis=-1))
        running_sum = running_sum * jnp.exp(running_max - new_max) + jnp.sum(
            jnp.exp(scores - new_max[..., None]), axis=-1
        )
        return (new_max, running_sum)

    start_max = jnp.full((kv_local, group_size, row_count), NEG_FILL, jnp.float32)
    start_sum = jnp.zeros((kv_local, group_size, row_count), jnp.float32)
    running_max, running_sum = lax.fori_loop(0, block_count, stat_step, (start_max, start_sum))
    log_total = running_max + jnp.log(running_sum)

    def out_step(block_id, out_sum):
        scores, _, value_block = block_scores(block_id)
        prob_low = jnp.exp(scores - log_total[..., None]).astype(jnp.bfloat16)
        return out_sum + jnp.einsum(
            "kgrc,ckd->rkgd", prob_low, value_block, preferred_element_type=jnp.float32
        )

    out_sum = lax.fori_loop(
        0,
        block_count,
        out_step,
        jnp.zeros((row_count, kv_local, group_size, head_size), jnp.float32),
    )
    out_low = out_sum.astype(jnp.bfloat16)
    delta_sum = jnp.transpose(
        jnp.sum(dout_rows.astype(jnp.float32) * out_low.astype(jnp.float32), axis=-1), (1, 2, 0)
    )

    def grad_step(block_id, carry):
        dq_sum, accumulator = carry
        scores, key_block, value_block = block_scores(block_id)
        probability = jnp.exp(scores - log_total[..., None])
        prob_low = probability.astype(jnp.bfloat16)
        dprob_full = jnp.einsum(
            "rkgd,ckd->kgrc", dout_rows, value_block, preferred_element_type=jnp.float32
        )
        dscore = (probability * (dprob_full - delta_sum[..., None])).astype(jnp.bfloat16)
        dq_sum = (
            dq_sum
            + jnp.einsum("kgrc,ckd->rkgd", dscore, key_block, preferred_element_type=jnp.float32)
            * scale_factor
        )
        dk_part = (
            jnp.einsum("kgrc,rkgd->ckd", dscore, query_rows, preferred_element_type=jnp.float32)
            * scale_factor
        )
        dv_part = jnp.einsum(
            "kgrc,rkgd->ckd", prob_low, dout_rows, preferred_element_type=jnp.float32
        )
        current = lax.dynamic_slice_in_dim(accumulator, block_id * block_size, block_size, 0)
        current = current + jnp.concatenate([dk_part, dv_part], -1)
        accumulator = lax.dynamic_update_slice_in_dim(
            accumulator, current, block_id * block_size, 0
        )
        return (dq_sum, accumulator)

    dq_start = jnp.zeros((row_count, kv_local, group_size, head_size), jnp.float32)
    dq_sum, accumulator = lax.fori_loop(0, block_count, grad_step, (dq_start, accumulator))
    return (out_low, dq_sum, accumulator)


def body(inputs, out_grad, w_query, w_key, w_value, w_output):
    tokens_dev = inputs.shape[0]
    kv_local = w_key.shape[1] // HD
    group_size = HQ // HK
    query_width = kv_local * group_size * HD
    key_width = kv_local * HD
    my_index = lax.axis_index("seq")
    first_row = my_index * tokens_dev
    positions = (first_row + jnp.arange(tokens_dev, dtype=jnp.int32)).astype(jnp.float32)
    cos_table, sin_table = rotary(positions)
    cos_heads, sin_heads = (cos_table[:, None, None, :], sin_table[:, None, None, :])
    queries = rotate(
        jnp.dot(inputs, w_query, preferred_element_type=jnp.float32).reshape(
            tokens_dev, kv_local, group_size, HD
        ),
        cos_heads,
        sin_heads,
    ).astype(jnp.bfloat16)
    key_rows = rotate(
        jnp.dot(inputs, w_key, preferred_element_type=jnp.float32).reshape(
            tokens_dev, kv_local, 1, HD
        ),
        cos_heads,
        sin_heads,
    ).reshape(tokens_dev, kv_local, HD)
    value_rows = jnp.dot(inputs, w_value, preferred_element_type=jnp.float32).reshape(
        tokens_dev, kv_local, HD
    )
    kv_own = jnp.concatenate([key_rows, value_rows], -1).astype(jnp.bfloat16)
    kv_all = lax.all_gather(kv_own, "seq", axis=0, tiled=True)
    grads_out = jnp.einsum(
        "td,fd->tf", out_grad, w_output, preferred_element_type=jnp.float32
    ).astype(jnp.bfloat16)
    grads_out = grads_out.reshape(tokens_dev, kv_local, group_size, HD)
    accumulator = jnp.zeros((kv_all.shape[0], kv_local, 2 * HD), jnp.float32)
    out_low, dq_sum, accumulator = attend(queries, grads_out, first_row, kv_all, accumulator)
    out_rows = out_low.reshape(tokens_dev, query_width)
    dq_rows = (
        unrotate(dq_sum, cos_heads, sin_heads).astype(jnp.bfloat16).reshape(tokens_dev, query_width)
    )
    kv_grads = lax.psum_scatter(accumulator, "seq", scatter_dimension=0, tiled=True)
    dk_rows = (
        unrotate(kv_grads[..., :HD], cos_table[:, None, :], sin_table[:, None, :])
        .astype(jnp.bfloat16)
        .reshape(tokens_dev, key_width)
    )
    dv_rows = kv_grads[..., HD:].astype(jnp.bfloat16).reshape(tokens_dev, key_width)
    local_grads = jnp.concatenate([dq_rows, dk_rows, dv_rows], 1)
    proj_part = jnp.einsum("tc,tf->cf", inputs, local_grads, preferred_element_type=jnp.float32)
    out_part = jnp.einsum("tc,tf->cf", out_grad, out_rows, preferred_element_type=jnp.float32)
    summed = lax.psum_scatter(
        jnp.concatenate([proj_part, out_part], 1), "seq", scatter_dimension=0, tiled=True
    )
    grad_query = summed[:, :query_width]
    grad_key = summed[:, query_width : query_width + key_width]
    grad_value = summed[:, query_width + key_width : query_width + 2 * key_width]
    grad_output = summed[:, query_width + 2 * key_width :].T
    input_term = jnp.einsum("tf,df->td", dq_rows, w_query, preferred_element_type=jnp.float32)
    input_term = input_term + jnp.einsum(
        "tf,df->td", dk_rows, w_key, preferred_element_type=jnp.float32
    )
    input_term = input_term + jnp.einsum(
        "tf,df->td", dv_rows, w_value, preferred_element_type=jnp.float32
    )
    grad_inputs = lax.psum_scatter(input_term, "head", scatter_dimension=1, tiled=True).astype(
        jnp.bfloat16
    )
    return (grad_inputs, grad_query, grad_key, grad_value, grad_output)


def solution(mesh):
    placed = (
        P("seq", None),
        P("seq", None),
        P(None, "head"),
        P(None, "head"),
        P(None, "head"),
        P("head", None),
    )
    return jax.shard_map(
        body,
        mesh=mesh,
        in_specs=placed,
        out_specs=(
            P("seq", "head"),
            P("seq", "head"),
            P("seq", "head"),
            P("seq", "head"),
            P("head", "seq"),
        ),
        check_vma=False,
    )
```

profile of v0, /device:TPU:2, one launch (start us, length us, event | category | flops | bytes accessed | tf_op | source)
XLA Modules:
  0.0 1038.6 jit_solution(18347865916576894489)
XLA Ops:
  7.3 1.5 copy-done
  8.8 1.7 fusion.46
  13.9 1.9 convolution_convert_fusion
  15.8 83.4 %all-gather.2.cloned.1.call-done = bf16[16384,1,128]{0,2,1:T(8,128)(2,1)} async-done(((bf16[512,1,128]{0,2,1:T(8,128)(2,1)}), bf16[16384,1,128]{0,2,1:T(8,128)(2,1)}) %all-gather.2.cloned.1.call-update) | async-done | bytes 4194320 | tf_op jit(solution)/shard_map/all_gather | solution.py:159
  99.2 20.1 %while.37 = (s32[]{:T(128)}, f32[1,2,512]{2,1,0:T(2,128)S(1)}, f32[1,2,512]{2,1,0:T(2,128)S(1)}, s32[]{:T(128)}, bf16[16384,1,128]{0,2,1:T(8,128)(2,1)}, /*index...) while((s32[]{:T(128)}, f32[1,2,512]{2,1,0:T(2,128)S(1)}, ...), condition=%wide.region_3.4_spmd.clone, body=%wide.region_0.3_spmd.clone.sunk | while | flops 71044104 | bytes 5238959 | solution.py:76
  99.5 1.4 fusion.115
  101.7 1.4 fusion.115
  103.9 1.4 fusion.115
  106.2 1.4 fusion.115
  108.4 1.4 fusion.115
  110.6 1.4 fusion.115
  112.9 1.4 fusion.115
  115.1 1.4 fusion.115
  117.3 1.4 fusion.115
  119.4 18.6 %while.38 = (s32[]{:T(128)}, f32[512,1,2,64]{0,3,2,1:T(8,128)S(1)}, s32[]{:T(128)}, bf16[16384,1,128]{0,2,1:T(8,128)(2,1)}, bf16[512,1,2,64]{0,3,2,1:T(8,128)(2,...) while((s32[]{:T(128)}, f32[512,1,2,64]{0,3,2,1:T(8,128)S(1)}, ...), condition=%wide.region_5.6_spmd.clone, body=%wide.region_4.5_spmd.clone.sunk | while | flops 136643584 | bytes 1324735 | solution.py:86
  119.6 1.8 fusion.117
  121.7 1.8 fusion.117
  123.7 1.8 fusion.117
  125.8 1.8 fusion.117
  127.9 1.8 fusion.117
  129.9 1.8 fusion.117
  132.0 1.8 fusion.117
  134.1 1.8 fusion.117
  136.1 1.8 fusion.117
  138.7 4.1 broadcast_in_dim.45
  142.8 82.3 %while.39 = (s32[]{:T(128)}, f32[512,1,2,64]{0,3,2,1:T(8,128)S(1)}, f32[16384,1,128]{0,2,1:T(8,128)}, s32[]{:T(128)}, bf16[16384,1,128]{0,2,1:T(8,128)(2,1)}, /*...) while((s32[]{:T(128)}, f32[512,1,2,64]{0,3,2,1:T(8,128)S(1)}, ...), condition=%wide.region_8.9_spmd.clone, body=%wide.region_7.8_spmd.clone.sunk | while | flops 339772416 | bytes 20660488 | solution.py:126
  143.0 2.9 fusion.125
  145.9 2.2 fusion.126
  150.2 1.7 fusion.129
  152.2 2.9 fusion.125
  155.1 2.2 fusion.126
  159.4 1.7 fusion.129
  161.3 2.9 fusion.125
  164.2 2.2 fusion.126
  168.5 1.7 fusion.129
  170.5 2.9 fusion.125
  173.4 2.2 fusion.126
  177.7 1.7 fusion.129
  179.6 2.9 fusion.125
  182.5 2.2 fusion.126
  186.8 1.7 fusion.129
  188.7 2.9 fusion.125
  191.6 2.2 fusion.126
  195.9 1.7 fusion.129
  197.9 2.9 fusion.125
  200.8 2.2 fusion.126
  205.1 1.7 fusion.129
  207.1 2.9 fusion.125
  210.0 2.2 fusion.126
  214.3 1.7 fusion.129
  216.2 2.9 fusion.125
  219.1 2.2 fusion.126
  223.4 1.7 fusion.129
  225.3 2.1 convolution_bitcast_fusion.3
  227.4 534.6 %reduce-scatter.6.cloned.1.call-done = f32[512,1,128]{0,2,1:T(8,128)} async-done(((f32[16384,1,128]{0,2,1:T(8,128)}), f32[512,1,128]{0,2,1:T(8,128)}) %reduce-scatter.6.cloned.1.call-update) | async-done | bytes 262160 | tf_op jit(solution)/shard_map/reduce_scatter | solution.py:170
  762.0 1.2 fusion.76
  764.9 1.9 pad_maximum_fusion
  766.7 3.6 copy.31
  773.1 2.7 add_add_fusion
  775.8 212.5 %reduce-scatter.10.cloned.1.call-done = f32[64,384]{1,0:T(8,128)} async-done(((f32[2048,384]{1,0:T(8,128)}), f32[64,384]{1,0:T(8,128)}) %reduce-scatter.10.cloned.1.call-update) | async-done | bytes 98320
  988.4 1.4 slice_bitcast_fusion
  989.8 1.5 fusion.79
  991.3 39.0 %reduce-scatter.8.cloned.1.call-done = f32[512,256]{1,0:T(8,128)} async-done(((f32[512,2048]{1,0:T(8,128)}), f32[512,256]{1,0:T(8,128)}) %reduce-scatter.8.cloned.1.call-update) | async-done | bytes 524304 | tf_op jit(solution)/shard_map/reduce_scatter | solution.py:194
  1030.3 1.8 convert_element_type.75
  (186 shorter events, 37.7 us)
Async XLA Ops:
  7.2 1.6 copy-start
  7.2 3.3 copy-start.5
  7.2 92.0 %all-gather.2.cloned.1.call-start = ((), (), s32[]{:S(2)}) async-start(), calls=%async_computation.3 | async-start | bytes 4325376 | tf_op jit(solution)/shard_map/all_gather | solution.py:159
  10.5 2.2 copy-start.3
  12.3 749.7 %reduce-scatter.6.cloned.1.call-start = ((), (), s32[]{:S(2)}) async-start(), calls=%async_computation.4 | async-start | bytes 8650752 | tf_op jit(solution)/shard_map/reduce_scatter | solution.py:170
  12.3 1.6 copy-start.2
  145.9 3.4 copy-start.1
  155.1 3.4 copy-start.1
  164.2 3.4 copy-start.1
  173.4 3.4 copy-start.1
  182.5 3.4 copy-start.1
  191.6 3.4 copy-start.1
  200.8 3.4 copy-start.1
  210.0 3.4 copy-start.1
  219.1 3.4 copy-start.1
  225.1 763.2 %reduce-scatter.10.cloned.1.call-start = ((), (), s32[]{:S(2)}) async-start(), calls=%async_computation.6 | async-start | bytes 3244032
  763.2 1.0 copy-start.8
  763.2 1.0 copy-start.10
  770.3 1.0 copy-start.4
  770.3 1.8 copy-start.9
  770.3 1.7 copy-start.11
  770.3 259.9 %reduce-scatter.8.cloned.1.call-start = ((), (), s32[]{:S(2)}) async-start(), calls=%async_computation.5 | async-start | bytes 4718592 | tf_op jit(solution)/shard_map/reduce_scatter | solution.py:194
  772.1 1.0 copy-start.6
  772.1 1.0 copy-start.7
Sparse Core Ops, SparseCore 0:
  12.4 86.7 all-gather.1
  225.3 536.6 reduce-scatter.5
  770.4 217.8 reduce-scatter.9
  990.8 39.4 reduce-scatter.7
where the time goes:
time: 1050 us; the launch traced here: 1040 us
  waiting for transfers between devices  870 us (83%)
  matrix products  106 us (10%)
  other arithmetic  33 us (3%)
  local copies, waits for them, and re-layouts  14.8 us (1%)
  between operations  14.1 us (1%)
    reduce_scatter x1, waiting for transfers between devices, body(): lax.psum_scatter(accumulator, 'seq', scatter_dimension=0, tiled=True)  535 us
    unnamed x5, waiting for transfers between devices  213 us
    all_gather x1, waiting for transfers between devices, body(): kv_all = lax.all_gather(kv_own, 'seq', axis=0, tiled=True)  83.4 us
    dot_general x18, matrix products, block_scores(): jnp.einsum('rkgd,ckd->kgrc', query_rows, key_block, preferred_element_typ...  39 us
    reduce_scatter x1, waiting for transfers between devices, body(): lax.psum_scatter(input_term, 'head', scatter_dimension=1, tiled=True)  39 us
  transfers between devices with their start and end apart: 4, of which 4 were waited for; matrix products, arithmetic and copies ran while one was open for 1% of the time, Pallas kernels for 0%

commit v1 on v0

v1 whole, which is shorter than its diff:
```python
import functools

import jax
import jax.numpy as jnp
from jax import lax
from jax.experimental import pallas as pl
from jax.experimental.pallas import tpu as pltpu
from jax.sharding import PartitionSpec as P

HD = 64
NX, NZ, NH = 4, 8, 8
ROPE_BASE = 500000.0
NEG = -1e30
F32, BF16 = jnp.float32, jnp.bfloat16
MESH = pl.DeviceIdType.MESH


def rotary(positions):
    half_dim = HD // 2
    frequency = ROPE_BASE ** (-(jnp.arange(half_dim, dtype=jnp.float32) * 2.0 / HD))
    angles = positions[:, None] * frequency[None, :]
    return jnp.cos(angles), jnp.sin(angles)


def mod(value, size):
    return lax.rem(value + 2 * size, size)


class Links:
    def __init__(self, send_sems, recv_sems):
        self.send_sems, self.recv_sems = send_sems, recv_sems
        self.used, self.open = 0, []

    def send(self, src, dst, device):
        index = self.used
        self.used += 1
        copy = pltpu.make_async_remote_copy(
            src_ref=src,
            dst_ref=dst,
            send_sem=self.send_sems.at[index],
            recv_sem=self.recv_sems.at[index],
            device_id=device,
            device_id_type=MESH,
        )
        copy.start()
        self.open.append(copy)
        return index

    def arrived(self, index, landing):
        pltpu.make_async_copy(landing, landing, self.recv_sems.at[index]).wait()

    def drain(self):
        for copy in self.open:
            copy.wait_send()
        self.open = []


def together(*streams):
    streams = list(streams)
    while streams:
        for stream in list(streams):
            try:
                next(stream)
            except StopIteration:
                streams.remove(stream)


def gather_ring(links, slots, own, where, size, right, left, cut):
    far = size // 2
    low, high = cut
    held_r, held_l = own, own
    for step in range(1, far + 1):
        slot_r, slot_l = mod(where - step + 1, size), mod(where + step - 1, size)
        if step == far:
            held_r, held_l = low(held_r), high(held_l)
            place_r, place_l = low(slots(slot_r)), high(slots(slot_l))
        else:
            place_r, place_l = slots(slot_r), slots(slot_l)
        got_r = links.send(held_r, place_r, right)
        got_l = links.send(held_l, place_l, left)
        yield
        held_r, held_l = slots(mod(where - step, size)), slots(mod(where + step, size))
        if step == far:
            links.arrived(got_r, low(held_r))
            links.arrived(got_l, high(held_l))
        else:
            links.arrived(got_r, held_r)
            links.arrived(got_l, held_l)


def scatter_ring(links, mine, snd, from_left, from_right, where, size, right, left, cut, finish):
    far = size // 2
    low, high = cut
    owner = mod(where + far, size)
    snd(owner)[...] = mine(owner)[...].astype(BF16)
    got_r = links.send(low(snd(owner)), low(from_left(0)), right)
    got_l = links.send(high(snd(owner)), high(from_right(0)), left)
    for step in range(2, far + 1):
        yield
        for got, came, place, sign, part, target in (
            (got_r, from_left, from_left, 1, low, right),
            (got_l, from_right, from_right, -1, high, left),
        ):
            owner = mod(where + sign * (far - step + 1), size)
            if step == 2:
                links.arrived(got, part(came(0)))
                other = high if part is low else low
                part(snd(owner))[...] = (
                    part(mine(owner))[...].astype(F32) + part(came(0))[...].astype(F32)
                ).astype(BF16)
                other(snd(owner))[...] = other(mine(owner))[...].astype(BF16)
            else:
                links.arrived(got, came(step - 2))
                snd(owner)[...] = (
                    mine(owner)[...].astype(F32) + came(step - 2)[...].astype(F32)
                ).astype(BF16)
            sent = links.send(snd(owner), place(step - 1), target)
            if sign == 1:
                got_r = sent
            else:
                got_l = sent
    yield
    links.arrived(got_r, from_left(far - 1))
    links.arrived(got_l, from_right(far - 1))
    finish(
        mine(where)[...].astype(F32)
        + from_left(far - 1)[...].astype(F32)
        + from_right(far - 1)[...].astype(F32)
    )


def seq_place():
    me = lax.axis_index("seq")
    return lax.div(me, NZ), lax.rem(me, NZ)


def seq_dev(x, z):
    return {"seq": x * NZ + z}


def greet(devices):
    barrier = pltpu.get_barrier_semaphore()
    for device in devices:
        pl.semaphore_signal(barrier, inc=1, device_id=device, device_id_type=MESH)
    pl.semaphore_wait(barrier, len(devices))


def nn(a, b):
    return lax.dot_general(a, b, (((1,), (0,)), ((), ())), preferred_element_type=F32)


def nt(a, b):
    return lax.dot_general(a, b, (((1,), (1,)), ((), ())), preferred_element_type=F32)


def attention_kernel(
    qd_own, kv_own, w_own,
    od_out, dkv_out, w_all,
    qd, kv, kvt, scores, probs, stats, o_sum, dq_sum, dkv,
    od, od_l, od_r, od_back, od_land, dkv_snd, dkv_l, dkv_r, dkv_back, dkv_land,
    send_sems, recv_sems, copy_sems,
):
    x, z = seq_place()
    head = lax.axis_index("head")
    chunk = kv_own.shape[1]
    lanes = qd_own.shape[2]
    right_x, left_x = seq_dev(mod(x + 1, NX), z), seq_dev(mod(x - 1, NX), z)
    across_x, mirror_x = seq_dev(mod(x + 2, NX), z), seq_dev(NX - 1 - x, z)
    right_z, left_z = seq_dev(x, mod(z + 1, NZ)), seq_dev(x, mod(z - 1, NZ))
    mirror_z = seq_dev(x, NZ - 1 - z)
    others = [{"head": mod(head + step, NH)} for step in range(1, NH)]
    greet([right_x, left_x, across_x, mirror_x, right_z, left_z, mirror_z] + others)
    links = Links(send_sems, recv_sems)

    sent = links.send(qd_own.at[1], qd.at[x, 1], mirror_z)
    sent_kv = links.send(kv_own.at[1], kv.at[z, 1], mirror_x)
    local = [
        pltpu.make_async_copy(qd_own.at[0], qd.at[x, 0], copy_sems.at[0]),
        pltpu.make_async_copy(kv_own.at[0], kv.at[z, 0], copy_sems.at[1]),
        pltpu.make_async_copy(w_own.at[head], w_all.at[head], copy_sems.at[2]),
    ]
    for copy in local:
        copy.start()
    rows_q = (lambda ref: ref.at[0:64], lambda ref: ref.at[64:128])
    rows_k = (lambda ref: ref.at[0 : chunk // 2], lambda ref: ref.at[chunk // 2 : chunk])

    def mirrored(index, landing, ring):
        yield
        links.arrived(index, landing)
        yield from ring

    together(
        gather_ring(links, lambda i: qd.at[i, 0], qd_own.at[0], x, NX, right_x, left_x, rows_q),
        gather_ring(links, lambda i: kv.at[i, 0], kv_own.at[0], z, NZ, right_z, left_z, rows_k),
        mirrored(sent, qd.at[x, 1],
                 gather_ring(links, lambda i: qd.at[i, 1], qd.at[x, 1], x, NX, right_x, left_x, rows_q)),
        mirrored(sent_kv, kv.at[z, 1],
                 gather_ring(links, lambda i: kv.at[i, 1], kv.at[z, 1], z, NZ, right_z, left_z, rows_k)),
    )
    for copy in local:
        copy.wait()
    weights = [
        (links.send(w_own.at[mod(head + step, NH)], w_all.at[head], others[step - 1]), step)
        for step in range(1, NH)
    ]

    def flip(index, _):
        i, a = lax.div(index, 2), lax.rem(index, 2)
        kvt[i, a] = kv[i, a].astype(F32).T.astype(BF16)
        dkv[i, a] = jnp.zeros(dkv.shape[2:], F32)
        return 0

    lax.fori_loop(0, 2 * NZ, flip, 0)

    def extents(group):
        i, a = lax.div(group, 2), lax.rem(group, 2)
        first = a == 0
        block = NZ * i + jnp.where(first, z, NZ - 1 - z)
        diag = jnp.where(first, (i == x).astype(jnp.int32), (i == NX - 1 - x).astype(jnp.int32))
        count_a = jnp.clip(block - NZ * x + 1, 0, NZ)
        count_b = jnp.clip(block - NZ * (NX - 1 - x) + a, 0, NZ)
        full_a = count_a - jnp.where(first, diag, 0)
        full_b = count_b - jnp.where(first, 0, diag)
        return i, a, full_a, full_a + full_b, diag

    def tile(k, full_a):
        in_a = k < full_a
        return jnp.where(in_a, k, k - full_a), jnp.where(in_a, 0, 1)

    def fold(values, op):
        return op(values.reshape(chunk // 8, 8, lanes), axis=0)

    def forward(group, offset):
        i, a, full_a, full, diag = extents(group)
        diag_z = jnp.where(a == 0, z, NZ - 1 - z)
        q_only = jnp.concatenate([qd[i, a, 0:64, :], jnp.zeros((64, lanes), BF16)], 0)

        def score(k, top):
            zc, ac = tile(k, full_a)
            s = nn(kv[zc, ac], q_only)
            scores[k] = s
            return jnp.maximum(top, fold(s, jnp.max))

        top = lax.fori_loop(0, full, score, jnp.full((8, lanes), NEG, F32))

        def score_diag(top):
            s = nn(kv[diag_z, a], q_only)
            key = lax.broadcasted_iota(jnp.int32, (chunk, lanes), 0)
            row = lax.rem(lax.broadcasted_iota(jnp.int32, (chunk, lanes), 1), chunk)
            s = jnp.where(row >= key, s, NEG)
            scores[full] = s
            return jnp.maximum(top, fold(s, jnp.max))

        top = lax.cond(diag == 1, score_diag, lambda t: t, top)
        top = jnp.max(top, axis=0, keepdims=True)
        o_sum[group] = jnp.zeros((64, lanes), F32)

        def weigh(k, total):
            zc, ac = tile(k, full_a)
            zc = jnp.where(k == full, diag_z, zc)
            ac = jnp.where(k == full, a, ac)
            p = jnp.exp(scores[k] - top)
            low = p.astype(BF16)
            probs[offset + k] = low
            o_sum[group] += nn(kvt[zc, ac, 64:128, :], low)
            return total + fold(p, jnp.sum)

        total = lax.fori_loop(0, full + diag, weigh, jnp.zeros((8, lanes), F32))
        dot_do = jnp.sum(o_sum[group] * qd[i, a, 64:128, :].astype(F32), axis=0, keepdims=True)
        stats[x, 0, pl.ds(group, 1), :] = top
        stats[x, 1, pl.ds(group, 1), :] = jnp.sum(total, axis=0, keepdims=True)
        stats[x, 2, pl.ds(group, 1), :] = dot_do
        return offset + full + diag

    lax.fori_loop(0, 2 * NX, forward, 0)

    shares = [
        (links.send(stats.at[x], stats.at[x], device), mod(x - step, NX))
        for step, device in ((1, right_x), (2, across_x), (3, left_x))
    ]
    for index, source in shares:
        links.arrived(index, stats.at[source])

    def backward(group, offset):
        i, a, full_a, full, diag = extents(group)
        diag_z = jnp.where(a == 0, z, NZ - 1 - z)
        tops = [stats[n, 0, pl.ds(group, 1), :] for n in range(NX)]
        top = functools.reduce(jnp.maximum, tops)
        weights_of = [jnp.exp(t - top) for t in tops]
        total = sum(stats[n, 1, pl.ds(group, 1), :] * weights_of[n] for n in range(NX))
        inverse = 1.0 / total
        delta = sum(stats[n, 2, pl.ds(group, 1), :] * weights_of[n] for n in range(NX)) * inverse
        scale = jnp.exp(stats[x, 0, pl.ds(group, 1), :] - top) * inverse
        blank = jnp.zeros((64, lanes), BF16)
        do = qd[i, a, 64:128, :]
        do_only = jnp.concatenate([blank, do], 0)
        q_scaled = jnp.concatenate([(qd[i, a, 0:64, :].astype(F32) * scale).astype(BF16), blank], 0)
        do_scaled = jnp.concatenate([blank, (do.astype(F32) * scale).astype(BF16)], 0)
        dq_sum[...] = jnp.zeros((64, lanes), F32)

        def step(k, _):
            zc, ac = tile(k, full_a)
            zc = jnp.where(k == full, diag_z, zc)
            ac = jnp.where(k == full, a, ac)
            p = probs[offset + k]
            dp = nn(kv[zc, ac], do_only)
            ds = (p.astype(F32) * (dp - delta)).astype(BF16)
            dkv[zc, ac] += nt(ds, q_scaled) + nt(p, do_scaled)
            dq_sum[...] += nn(kvt[zc, ac, 0:64, :], ds)
            return 0

        lax.fori_loop(0, full + diag, step, 0)
        od[i, a, 0:64, :] = (o_sum[group] * scale).astype(BF16)
        od[i, a, 64:128, :] = (dq_sum[...] * (scale * 0.125)).astype(BF16)
        return offset + full + diag

    lax.fori_loop(0, 2 * NX, backward, 0)

    pair_q = (lambda ref: ref.at[:, 0:64], lambda ref: ref.at[:, 64:128])
    pair_k = (lambda ref: ref.at[:, 0 : chunk // 2], lambda ref: ref.at[:, chunk // 2 : chunk])

    def finish_od(value):
        od_out[0] = value[0].astype(BF16)
        od_back[...] = value[1].astype(BF16)

    def finish_dkv(value):
        dkv_out[0] = value[0]
        dkv_back[...] = value[1].astype(BF16)

    together(
        scatter_ring(links, lambda i: od.at[i], lambda i: od.at[i], lambda i: od_l.at[i], lambda i: od_r.at[i],
                     x, NX, right_x, left_x, pair_q, finish_od),
        scatter_ring(links, lambda i: dkv.at[i], lambda i: dkv_snd.at[i], lambda i: dkv_l.at[i],
                     lambda i: dkv_r.at[i], z, NZ, right_z, left_z, pair_k, finish_dkv),
    )
    got_od = links.send(od_back, od_land, mirror_z)
    got_dkv = links.send(dkv_back, dkv_land, mirror_x)
    links.arrived(got_od, od_land)
    links.arrived(got_dkv, dkv_land)
    od_out[1] = od_land[...]
    dkv_out[1] = dkv_land[...].astype(F32)
    for index, step in weights:
        links.arrived(index, w_all.at[mod(head - step, NH)])
    links.drain()


def attention(qd_own, kv_own, w_own):
    chunk, lanes = kv_own.shape[1], qd_own.shape[2]
    tiles = (2 * NX * 2 * NZ) // 2 + 1
    vmem = pl.BlockSpec(memory_space=pltpu.VMEM)
    anywhere = pl.BlockSpec(memory_space=pl.ANY)
    copies = 56
    return pl.pallas_call(
        attention_kernel,
        out_shape=(
            jax.ShapeDtypeStruct((2, 128, lanes), BF16),
            jax.ShapeDtypeStruct((2, chunk, 128), F32),
            jax.ShapeDtypeStruct(w_own.shape, BF16),
        ),
        in_specs=[vmem, vmem, anywhere],
        out_specs=(vmem, vmem, anywhere),
        scratch_shapes=[
            pltpu.VMEM((NX, 2, 128, lanes), BF16),
            pltpu.VMEM((NZ, 2, chunk, 128), BF16),
            pltpu.VMEM((NZ, 2, 128, chunk), BF16),
            pltpu.VMEM((2 * NZ, chunk, lanes), F32),
            pltpu.VMEM((tiles, chunk, lanes), BF16),
            pltpu.VMEM((NX, 3, 8, lanes), F32),
            pltpu.VMEM((2 * NX, 64, lanes), F32),
            pltpu.VMEM((64, lanes), F32),
            pltpu.VMEM((NZ, 2, chunk, 128), F32),
            pltpu.VMEM((NX, 2, 128, lanes), BF16),
            pltpu.VMEM((NX // 2, 2, 128, lanes), BF16),
            pltpu.VMEM((NX // 2, 2, 128, lanes), BF16),
            pltpu.VMEM((128, lanes), BF16),
            pltpu.VMEM((128, lanes), BF16),
            pltpu.VMEM((NZ, 2, chunk, 128), BF16),
            pltpu.VMEM((NZ // 2, 2, chunk, 128), BF16),
            pltpu.VMEM((NZ // 2, 2, chunk, 128), BF16),
            pltpu.VMEM((chunk, 128), BF16),
            pltpu.VMEM((chunk, 128), BF16),
            pltpu.SemaphoreType.DMA((copies,)),
            pltpu.SemaphoreType.DMA((copies,)),
            pltpu.SemaphoreType.DMA((3,)),
        ],
        compiler_params=pltpu.CompilerParams(
            collective_id=0, has_side_effects=True, vmem_limit_bytes=56 * 1024 * 1024
        ),
        name="attention",
    )(qd_own, kv_own, w_own)


def finish_kernel(
    g_own, proj, outp,
    g_all, proj_out, outp_out,
    proj_snd, proj_l, proj_r, proj_z, projz_snd, projz_l, projz_r,
    outp_snd, outp_l, outp_r, outp_x, outpx_snd, outpx_l, outpx_r,
    send_sems, recv_sems, copy_sem,
):
    x, z = seq_place()
    head = lax.axis_index("head")
    y, core = lax.div(head, 2), lax.rem(head, 2)
    right_x, left_x = seq_dev(mod(x + 1, NX), z), seq_dev(mod(x - 1, NX), z)
    right_z, left_z = seq_dev(x, mod(z + 1, NZ)), seq_dev(x, mod(z - 1, NZ))
    right_y, left_y = {"head": mod(y + 1, 4) * 2 + core}, {"head": mod(y - 1, 4) * 2 + core}
    twin = {"head": y * 2 + 1 - core}
    greet([right_x, left_x, right_z, left_z, right_y, left_y, twin])
    links = Links(send_sems, recv_sems)
    keep = pltpu.make_async_copy(g_own, g_all.at[head], copy_sem)
    keep.start()

    def slot(i, c):
        return g_all.at[i * 2 + c]

    def spread():
        rows = g_own.shape[0] // 2
        cut = (lambda ref: ref.at[0:rows], lambda ref: ref.at[rows : 2 * rows])
        ring = gather_ring(links, lambda i: slot(i, core), g_own, y, 4, right_y, left_y, cut)
        next(ring)
        got = [(links.send(g_own, slot(y, core), twin), y)]
        yield
        next(ring)
        for i in (mod(y - 1, 4), mod(y + 1, 4)):
            got.append((links.send(slot(i, core), slot(i, core), twin), i))
        yield
        for _ in ring:
            pass
        i = mod(y + 2, 4)
        got.append((links.send(slot(i, core), slot(i, core), twin), i))
        yield
        for index, i in got:
            links.arrived(index, slot(i, 1 - core))

    def halves(dim, size):
        low, high = slice(0, size // 2), slice(size // 2, size)
        if dim == 0:
            return (lambda ref: ref.at[low], lambda ref: ref.at[high])
        return (lambda ref: ref.at[:, low], lambda ref: ref.at[:, high])

    slab = proj.shape[2]

    def keep_to(ref):
        def write(value):
            ref[...] = value.astype(ref.dtype)

        return write

    def proj_sums():
        yield from scatter_ring(
            links, lambda i: proj.at[i], lambda i: proj_snd.at[i], lambda i: proj_l.at[i], lambda i: proj_r.at[i],
            x, NX, right_x, left_x, halves(0, NZ), keep_to(proj_z))
        yield from scatter_ring(
            links, lambda i: proj_z.at[i], lambda i: projz_snd.at[i], lambda i: projz_l.at[i], lambda i: projz_r.at[i],
            z, NZ, right_z, left_z, halves(0, slab), keep_to(proj_out))

    def outp_sums():
        yield from scatter_ring(
            links, lambda i: outp.at[:, i], lambda i: outp_snd.at[i], lambda i: outp_l.at[i], lambda i: outp_r.at[i],
            z, NZ, right_z, left_z, halves(0, NX), keep_to(outp_x))
        yield from scatter_ring(
            links, lambda i: outp_x.at[i], lambda i: outpx_snd.at[i], lambda i: outpx_l.at[i], lambda i: outpx_r.at[i],
            x, NX, right_x, left_x, halves(0, slab), keep_to(outp_out))

    together(proj_sums(), outp_sums(), spread())
    keep.wait()
    links.drain()


def finish(g_own, proj, outp):
    vmem = pl.BlockSpec(memory_space=pltpu.VMEM)
    _, _, slab, wide = proj.shape
    narrow = outp.shape[3]
    copies = 48

    def vm(*shape, dtype=BF16):
        return pltpu.VMEM(shape, dtype)

    return pl.pallas_call(
        finish_kernel,
        out_shape=(
            jax.ShapeDtypeStruct((NH,) + g_own.shape, BF16),
            jax.ShapeDtypeStruct((slab, wide), F32),
            jax.ShapeDtypeStruct((slab, narrow), F32),
        ),
        in_specs=[vmem] * 3,
        out_specs=(vmem,) * 3,
        scratch_shapes=[
            vm(NX, NZ, slab, wide), vm(NX // 2, NZ, slab, wide), vm(NX // 2, NZ, slab, wide),
            vm(NZ, slab, wide, dtype=F32), vm(NZ, slab, wide), vm(NZ // 2, slab, wide), vm(NZ // 2, slab, wide),
            vm(NZ, NX, slab, narrow), vm(NZ // 2, NX, slab, narrow), vm(NZ // 2, NX, slab, narrow),
            vm(NX, slab, narrow, dtype=F32), vm(NX, slab, narrow), vm(NX // 2, slab, narrow), vm(NX // 2, slab, narrow),
            pltpu.SemaphoreType.DMA((copies,)),
            pltpu.SemaphoreType.DMA((copies,)),
            pltpu.SemaphoreType.DMA,
        ],
        compiler_params=pltpu.CompilerParams(
            collective_id=1, has_side_effects=True, vmem_limit_bytes=40 * 1024 * 1024
        ),
        name="finish",
    )(g_own, proj, outp)


def body(inputs, out_grad, w_query, w_key, w_value, w_output):
    tokens = inputs.shape[0]
    chunk = tokens // 2
    model = inputs.shape[1]
    me = lax.axis_index("seq")
    positions = (me * tokens + jnp.arange(tokens, dtype=jnp.int32)).astype(F32)
    cos, sin = rotary(positions)
    cos_t, sin_t = cos.T, sin.T

    q = jnp.einsum("td,df->ft", inputs, w_query, preferred_element_type=F32).reshape(2, HD, tokens)
    front, back = q[:, :32], q[:, 32:]
    q = jnp.concatenate([front * cos_t - back * sin_t, back * cos_t + front * sin_t], 1).astype(BF16)
    q = q * jnp.asarray(0.125, BF16)
    do = jnp.einsum("td,fd->ft", out_grad, w_output, preferred_element_type=F32).astype(BF16)
    qd = jnp.concatenate([q, do.reshape(2, HD, tokens)], 1)
    qd = qd.reshape(2, 128, 2, chunk).transpose(2, 1, 0, 3).reshape(2, 128, 2 * chunk)
    k = jnp.dot(inputs, w_key, preferred_element_type=F32)
    front, back = k[:, :32], k[:, 32:]
    k = jnp.concatenate([front * cos - back * sin, back * cos + front * sin], 1)
    v = jnp.dot(inputs, w_value, preferred_element_type=F32)
    kv = jnp.concatenate([k, v], 1).astype(BF16).reshape(2, chunk, 128)
    w_own = jnp.concatenate([w_query, w_key, w_value], 1).reshape(NH, model // NH, 256)

    od, dkv, w_all = attention(qd, kv, w_own)

    od = od.reshape(2, 2, HD, 2, chunk)
    od = od.transpose(1, 3, 2, 0, 4).reshape(2, 2, HD, tokens)
    o = od[0].reshape(128, tokens)
    dq = od[1].astype(F32)
    front, back = dq[:, :32], dq[:, 32:]
    dq = jnp.concatenate([front * cos_t + back * sin_t, back * cos_t - front * sin_t], 1)
    dq = dq.astype(BF16).reshape(128, tokens).T
    dkv = dkv.reshape(tokens, 128)
    front, back = dkv[:, :32], dkv[:, 32:64]
    g = jnp.concatenate(
        [
            dq,
            (front * cos + back * sin).astype(BF16),
            (back * cos - front * sin).astype(BF16),
            dkv[:, 64:].astype(BF16),
        ],
        1,
    )
    slab = model // (NX * NZ)
    proj = jnp.einsum("tc,tf->cf", inputs, g, preferred_element_type=F32).astype(BF16)
    outp = jnp.einsum("tc,ft->cf", out_grad, o, preferred_element_type=F32).astype(BF16)
    g_all, proj_sum, outp_sum = finish(
        g, proj.reshape(NX, NZ, slab, 256), outp.reshape(NX, NZ, slab, 128)
    )
    grad_inputs = jnp.einsum("htf,hcf->tc", g_all, w_all, preferred_element_type=F32).astype(BF16)
    return grad_inputs, proj_sum[:, :128], proj_sum[:, 128:192], proj_sum[:, 192:], outp_sum.T


def solution(mesh):
    placed = (
        P("seq", None),
        P("seq", None),
        P(None, "head"),
        P(None, "head"),
        P(None, "head"),
        P("head", None),
    )
    return jax.shard_map(
        body,
        mesh=mesh,
        in_specs=placed,
        out_specs=(
            P("seq", "head"),
            P("seq", "head"),
            P("seq", "head"),
            P("seq", "head"),
            P("head", "seq"),
        ),
        check_vma=False,
    )
```

time: 1050 us -> 185 us (0.18); the launches traced: 1040 us -> 185 us
  waiting for transfers between devices: 870 us -> 0 us
  Pallas kernels: 0 us -> 153 us
  matrix products: 106 us -> 12.1 us
  other arithmetic: 33 us -> 7.86 us
  between operations: 14.1 us -> 0.94 us
    reduce_scatter x2 -> x0, waiting for transfers between devices: 574 us -> none  [the longest x1 535 us: body(): lax.psum_scatter(accumulator, 'seq', scatter_dimension=0, tiled=True)]
    unnamed x5 -> x0, waiting for transfers between devices: 213 us -> none
    pallas_call x0 -> x2, Pallas kernels: none -> 153 us  [the longest x1 121 us: attention(): pl.pallas_call(attention_kernel, out_shape=(jax.ShapeDtypeStruct((2, 128,...]
    dot_general x72 -> x7, matrix products: 106 us -> 12.1 us  [the longest x1 2.67 us: body(): jnp.einsum('htf,hcf->tc', g_all, w_all, preferred_element_type=F32)]
    all_gather x1 -> x0, waiting for transfers between devices: 83.4 us -> none  [body(): kv_all = lax.all_gather(kv_own, 'seq', axis=0, tiled=True)]
    dynamic_update_slice x9 -> x0, other arithmetic: 15.4 us -> none  [grad_step(): lax.dynamic_update_slice_in_dim(accumulator, current, block_id * block_si...]
  transfers between devices with their start and end apart: 4 -> 0, of which waited for: 4 -> 0; matrix products, arithmetic and copies ran while one was open for 1% -> 0% of each run, Pallas kernels for 0% -> 0%
where the time goes in v1:
time: 185 us
  Pallas kernels  153 us (83%)
  matrix products  12.1 us (7%)
  local copies, waits for them, and re-layouts  11.6 us (6%)
  other arithmetic  7.86 us (4%)
    pallas_call x1, Pallas kernels, attention(): pl.pallas_call(attention_kernel, out_shape=(jax.ShapeDtypeStruct((2, 128,...  121 us
    pallas_call x1, Pallas kernels, finish(): pl.pallas_call(finish_kernel, out_shape=(jax.ShapeDtypeStruct((NH,) + g_o...  31.1 us
    unnamed x16, local copies, waits for them, and re-layouts  3.78 us

profile of v1, /device:TPU:2, one launch (start us, length us, event | category | flops | bytes accessed | tf_op | source)
XLA Modules:
  0.0 185.0 jit_solution(8518224543329050912)
XLA Ops:
  0.6 0.0 copy-start
  0.6 0.0 copy-start.5
  0.7 1.5 copy-done
  2.2 1.7 convolution_convert_fusion.3
  3.9 0.0 copy-start.2
  3.9 0.1 copy.42
  4.1 0.0 copy-done.5
  4.1 2.5 %convolution_convert_fusion.2 = bf16[128,512]{1,0:T(8,128)(2,1)S(1)} fusion(bf16[128,2048]{1,0:T(8,128)(2,1)S(1)} %copy-done.5, bf16[512,2048]{1,0:T(8,128)(2,1)} %param.7), kind=kOutput, calls=%fused_computation.6 | convolution fusion | flops 268500992 | bytes 2752512 | tf_op jit(solution)/shard_map/td,fd->ft/dot_general | solution.py:516
  6.6 0.1 copy.38
  6.7 0.3 multiply_cosine_fusion.1
  7.0 0.0 copy-done.2
  7.1 0.0 copy-start.3
  7.1 0.8 fusion.21
  8.0 0.1 copy.36
  8.1 0.1 copy.37
  8.1 0.2 maximum_multiply_fusion
  8.3 0.3 maximum_bitcast_fusion
  8.7 0.9 reshape.122.qd_own
  9.6 0.0 copy-done.3
  9.6 0.0 copy-start.4
  9.6 0.7 fusion.22
  10.3 1.2 fusion.12
  11.5 0.8 pad_maximum_fusion.2.kv_own
  12.3 0.3 copy.43
  12.6 0.0 copy-done.4
  12.6 0.3 copy.44
  12.9 2.4 %pad_maximum_fusion = bf16[2048,256]{1,0:T(8,128)(2,1)} fusion(bf16[2048,64]{1,0:T(8,128)(2,1)S(1)} %copy.44, bf16[2048,64]{1,0:T(8,128)(2,1)S(1)} %copy.43, bf16[2048,128]{1,0:T(8,128)(2,1)} %param.8), kind=kLoop, calls=%fused_computation.8 | loop fusion | flops 3145728 | bytes 2097152 | tf_op jit(solution)/shard_map/concatenate | solution.py:524
  15.2 121.4 %attention.1 = (bf16[2,128,512]{2,1,0:T(8,128)(2,1)}, f32[2,256,128]{2,1,0:T(8,128)}, bf16[8,256,256]{2,1,0:T(8,128)(2,1)}) custom-call(bf16[2,128,512]{2,1,0:T(8,128)(2,1)} %reshape.122.qd_own, bf16[2,256,128]{2,1,0:T(8,128)(2,1)} %pad_maximum_fusion.2.kv_own, bf16[8,256,256]{2,1,0:T(8,128)(2,1)} %bitcast.44), custom_call_target="tpu_custom_call" | custom-call | tf_op jit(solution)/shard_map/attention/pallas_call | solution.py:353
  136.7 1.0 reshape.124
  137.7 0.3 copy.52
  137.9 1.0 slice.88
  139.0 2.2 %fusion.16 = (bf16[512,32]{1,0:T(8,128)(2,1)S(1)}, bf16[512,32]{1,0:T(8,128)(2,1)S(1)}) fusion(f32[512,128]{1,0:T(8,128)} %bitcast.46, f32[512]{0:T(512)S(1)} %add_convert_fusion.2, f32[32]{0:T(128)S(1)} %negate_power_fusion), kind=kLoop, calls=%fused_computation.24 | loop fusion | flops 147456 | bytes 198784 | tf_op jit(solution)/shard_map/convert_element_type | solution.py:540
  141.2 0.2 fusion.19
  141.4 0.2 reshape.128
  141.7 0.1 copy.46
  141.8 0.1 pad_maximum_fusion.1.g_own
  142.0 2.0 %fusion.1 = bf16[2048,128]{0,1:T(8,128)(2,1)S(1)} fusion(bf16[128,512]{1,0:T(8,128)(2,1)S(1)} %bitcast.55, bf16[512,2048]{1,0:T(8,128)(2,1)} %param.7), kind=kOutput, calls=%fused_computation.3 | convolution fusion | flops 268697600 | bytes 2752512 | tf_op jit(solution)/shard_map/tc,ft->cf/dot_general | solution.py:548
  144.0 1.0 copy.48
  145.0 1.7 fusion
  146.8 1.5 copy.47
  148.3 0.0 copy-start.1
  148.3 1.0 copy-done.1
  149.3 31.1 %finish.1 = (bf16[8,512,256]{2,1,0:T(8,128)(2,1)S(1)}, f32[64,256]{1,0:T(8,128)S(1)}, f32[64,128]{1,0:T(8,128)S(1)}) custom-call(bf16[512,256]{1,0:T(8,128)(2,1)S(1)} %pad_maximum_fusion.1.g_own, bf16[4,8,64,256]{3,2,1,0:T(8,128)(2,1)S(1)} %bitcast.41, bf16[4,8,64,128]{3,2,1,0:T(8,128)(2,1)S(1)} %bitcast.42), custom_call_target="tpu_custom_call" | custom-call | tf_op jit(solution)/shard_map/finish/pallas_call | solution.py:478
  180.4 2.7 %fusion.2 = bf16[512,256]{1,0:T(8,128)(2,1)} fusion(bf16[8,512,256]{2,1,0:T(8,128)(2,1)S(1)} %get-tuple-element.13, bf16[8,256,256]{2,1,0:T(8,128)(2,1)} %get-tuple-element.14), kind=kOutput, calls=%fused_computation.5 | convolution fusion | flops 537001984 | bytes 3407872 | tf_op jit(solution)/shard_map/htf,hcf->tc/dot_general | solution.py:552
  183.1 0.6 slice.56
  183.7 0.7 fusion.20
  184.4 0.6 copy.54
  (9 shorter events, 0.2 us)
Async XLA Ops:
  0.6 1.6 copy-start
  0.6 3.4 %copy-start.5 = (bf16[128,2048]{1,0:T(8,128)(2,1)S(1)}, bf16[128,2048]{1,0:T(8,128)(2,1)}, u32[]{:S(2)}) copy-start(bf16[128,2048]{1,0:T(8,128)(2,1)} %param.11) | copy-start | bytes 1572868
  3.9 3.1 %copy-start.2 = (bf16[2048,128]{1,0:T(8,128)(2,1)S(1)}, bf16[2048,128]{1,0:T(8,128)(2,1)}, u32[]{:S(2)}) copy-start(bf16[2048,128]{1,0:T(8,128)(2,1)} %param.8) | copy-start | bytes 1572868
  7.1 2.5 %copy-start.3 = (bf16[2048,64]{0,1:T(8,128)(2,1)S(1)}, bf16[2048,64]{0,1:T(8,128)(2,1)}, u32[]{:S(2)}) copy-start(bf16[2048,64]{0,1:T(8,128)(2,1)} %param.9) | copy-start | bytes 786436
  9.6 3.0 %copy-start.4 = (bf16[2048,64]{0,1:T(8,128)(2,1)S(1)}, bf16[2048,64]{0,1:T(8,128)(2,1)}, u32[]{:S(2)}) copy-start(bf16[2048,64]{0,1:T(8,128)(2,1)} %param.10) | copy-start | bytes 786436
  148.3 1.0 copy-start.1
